TPU v7x, 32 devices: a whole 2x2x4 slice. The times are simulated.
32 devices in a mesh: tm: 8 (over z, x), gz: 4 (over y, core).
Axes of the slice: x: 2, y: 2, z: 4, core: 2. Of those that a mesh axis runs over, the one named last changes fastest.
Arguments:
- states: float32 [8, 3, 64, 16, 128], P('tm', None, 'gz'), may hold values from -4 to 4
- rate: float32 [64, 16, 128], P('gz'), may hold values from 0.1 to 40
Outputs:
- new_states: float32 [8, 3, 64, 16, 128], P('tm', None, 'gz')
All inputs are finite; a program needn't handle non-finite values.
Results may differ from a plain program's by a relative error of at most 0.000044.
Values sent between devices are 32-bit elements; how exact they have to be, the bound alone decides.
No kernel may reach another device: no remote copies, remote signals or barrier semaphores. Data moves between devices by JAX's collectives and lax.ppermute only.
A program may use at most 128 MiB of HBM per device.

v0:
```python
import functools

import jax
import jax.numpy as jnp
from jax import lax
from jax.experimental import pallas as pl
from jax.experimental.pallas import tpu as pltpu
from jax.sharding import PartitionSpec as P

STEPS = 2
STAGES = 3 * STEPS
GROUP = 4
VISCOSITY = 0.05
TIME_STEP = 0.2
MIX = ((1.0, None), (0.25, 0.75), (2.0 / 3.0, 1.0 / 3.0))
VMEM = pl.BlockSpec(memory_space=pltpu.VMEM)
PARAMS = pltpu.CompilerParams(vmem_limit_bytes=16 * 1024 * 1024)


def call(kernel, out_shape, *args, scratch=(), flops=None):
    cost = None
    if flops is not None:
        cost = pl.CostEstimate(flops=flops, bytes_accessed=1 << 20, transcendentals=0)
    return pl.pallas_call(
        kernel,
        out_shape=out_shape,
        in_specs=[VMEM] * len(args),
        out_specs=jax.tree.map(lambda _: VMEM, out_shape),
        scratch_shapes=list(scratch),
        compiler_params=PARAMS,
        cost_estimate=cost,
    )(*args)


def f32(*shape):
    return jax.ShapeDtypeStruct(shape, jnp.float32)


def partner(k):
    return (GROUP - k) % GROUP


def spot():
    return lax.rem(lax.axis_index("tm"), GROUP)


def chunk_of(k):
    flip = 2 * lax.rem(lax.axis_index("tm") // GROUP, 2)
    return lax.bitwise_xor(lax.bitwise_xor(spot(), flip), partner(k))


def near_side():
    return 1 - lax.rem(lax.axis_index("gz"), 2)


def split_rows(ref, *lead):
    half = ref.shape[-2] // 2
    return [ref[(*lead, pl.ds(odd, half, stride=2), slice(None))] for odd in (0, 1)]


def join_rows(ref, lead, pair):
    half = ref.shape[-2] // 2
    for odd in (0, 1):
        ref[(*lead, pl.ds(odd, half, stride=2), slice(None))] = pair[odd]


def load(ref, *lead):
    return [[ref[(*lead, c, odd)] for odd in (0, 1)] for c in range(3)]


def store(ref, lead, value):
    for c in range(3):
        for odd in (0, 1):
            ref[(*lead, c, odd)] = value[c][odd]


def advance(last, here, ahead, alpha, upward=1.0):
    diffuse = alpha * TIME_STEP * VISCOSITY
    carry = alpha * TIME_STEP * 0.5
    result = [[None, None] for _ in range(3)]
    for odd in (0, 1):
        speed = [here[0][odd] * carry, here[1][odd] * carry, here[2][odd] * (carry * upward)]
        to_next = [diffuse - s for s in speed]
        to_last = [diffuse + s for s in speed]
        for c in range(3):
            w = here[c][odd]
            rows, width = w.shape
            other = here[c][1 - odd]
            if odd:
                y_next, y_last = pltpu.roll(other, rows - 1, 0), other
            else:
                y_next, y_last = other, pltpu.roll(other, 1, 0)
            total = (alpha - 6.0 * diffuse) * w
            total = total + (
                to_next[0] * pltpu.roll(w, width - 1, 1) + to_last[0] * pltpu.roll(w, 1, 1)
            )
            total = total + (to_next[1] * y_next + to_last[1] * y_last)
            total = total + (to_next[2] * ahead[c][odd] + to_last[2] * last[c][odd])
            result[c][odd] = total
    return result


def blend(new, beta, base):
    return [[new[c][odd] + beta * base[c][odd] for odd in (0, 1)] for c in range(3)]


def faces_kernel(own_ref, far_ref, near_ref):
    layers, width = own_ref.shape[1], near_ref.shape[1]
    near = near_side()
    top = layers - width
    far_ref[...] = own_ref[:, pl.ds((1 - near) * top, width)]
    near_ref[...] = own_ref[:, pl.ds(near * top, width)]


def inside_kernel(own_ref, rate_ref, edges, middle, faded, damp_ref, damps, *fields):
    layers = own_ref.shape[1]
    half = layers // 2
    slices = lax.axis_size("tm")
    keep = (lax.axis_index("tm") != 0).astype(jnp.float32)

    def fill(z, _):
        for c in range(3):
            for odd, value in enumerate(split_rows(own_ref, c, z)):
                fields[0][z, c, odd] = value
        return 0

    lax.fori_loop(0, layers, fill, 0, unroll=2)

    def save(stage, field):
        for j in range(3):
            store(edges, (stage, 0, j), load(field, stage + j))
            store(edges, (stage, 1, j), load(field, layers - 1 - stage - j))

    def sweep(stage, source, target, base, alpha, beta):
        def body(turn, carry):
            below, here = carry
            for k in range(2):
                z = stage + 2 * turn + k
                above = load(source, z + 1)
                new = advance(below, here, above, alpha)
                if beta is not None:
                    new = blend(new, beta, load(base, z))
                store(target, (z,), new)
                below, here = here, above
            return below, here

        first = (load(source, stage - 1), load(source, stage))
        lax.fori_loop(0, (layers - 2 * stage) // 2, body, first)

    save(0, fields[0])
    for stage in range(1, STAGES + 1):
        kind = (stage - 1) % 3
        target = fields[(kind + 1) % 3]
        sweep(stage, fields[kind], target, fields[0], *MIX[kind])
        if stage < STAGES:
            save(stage, target)

    for z in range(layers):
        side, slot = (0, z) if z < half else (1, layers - 1 - z)
        damp = [jnp.exp(r * (-1.0 / slices)) for r in split_rows(rate_ref, z)]
        for odd in (0, 1):
            damps[side, slot, odd] = damp[odd]
        for c in range(3):
            start = split_rows(own_ref, c, z)
            for odd in (0, 1):
                lost = damp[odd] * keep * start[odd]
                if slot < STAGES:
                    faded[side, slot, c, odd] = lost
                else:
                    middle[side, slot - STAGES, c, odd] = fields[0][z, c, odd] - lost

    share = layers // GROUP
    chunk, near = chunk_of(0), near_side()
    side = jnp.where(chunk < GROUP // 2, near, 1 - near)
    damp_ref[...] = damps[side, pl.ds(lax.rem(chunk, 2) * share, share)]


def border(side, face_ref, edges, middle, faded, jumps, strip):
    width = STAGES
    upward = 1.0 - 2.0 * side.astype(jnp.float32)
    for slot in range(width):
        layer = slot + side * (width - 1 - 2 * slot)
        for c in range(3):
            for odd, value in enumerate(split_rows(face_ref, c, layer)):
                strip[0, slot, c, odd] = value

    def at(stage, slot):
        if slot < width:
            return load(strip, stage, slot)
        return load(edges, stage, side, slot - width)

    def step(turn, _):
        for kind, (alpha, beta) in enumerate(MIX):
            stage = 3 * turn + kind
            last, here = at(stage, 0), at(stage, 1)
            for slot in range(width):
                ahead = at(stage, slot + 2)
                new = advance(last, here, ahead, alpha, upward)
                if beta is not None:
                    new = blend(new, beta, at(3 * turn, slot + 1 + kind))
                store(strip, (stage + 1, slot), new)
                last, here = here, ahead
        return 0

    lax.fori_loop(0, STEPS, step, 0)
    for slot in range(jumps.shape[0]):
        if slot < width:
            end, lost = load(strip, STAGES, slot), load(faded, side, slot)
            store(jumps, (slot,), [[end[c][odd] - lost[c][odd] for odd in (0, 1)] for c in range(3)])
        else:
            store(jumps, (slot,), load(middle, side, slot - width))


def near_kernel(face_ref, edges, middle, faded, jumps, strip):
    border(near_side(), face_ref, edges, middle, faded, jumps, strip)


def far_kernel(face_ref, edges, middle, faded, near_jumps, *refs):
    outs, strip, jumps = refs[:GROUP], refs[GROUP], refs[GROUP + 1]
    border(1 - near_side(), face_ref, edges, middle, faded, jumps.at[1], strip)
    jumps[0] = near_jumps[...]
    share = outs[0].shape[0]
    for k, out in enumerate(outs):
        chunk = chunk_of(k)
        out[...] = jumps[chunk // 2, pl.ds(lax.rem(chunk, 2) * share, share)]


def sort_in(jumps, order):
    for k in range(GROUP):
        order[lax.bitwise_xor(spot(), partner(k))] = jumps[k][...]


def sort_out(order, outs):
    for k in range(GROUP):
        outs[k][...] = order[lax.bitwise_xor(spot(), partner(k))]


def run(order, damp, total):
    for j in range(GROUP):
        jump = order[j]
        order[j] = total
        total = damp * total + jump
    return total


def total_kernel(*refs):
    jumps, damp_ref, out, order = refs[:GROUP], refs[GROUP], refs[GROUP + 1], refs[GROUP + 2]
    sort_in(jumps, order)
    out[...] = run(order, damp_ref[...][:, None], jnp.zeros(out.shape, jnp.float32))


def spread_kernel(*refs):
    carry_ref, jumps, damp_ref = refs[0], refs[1 : 1 + GROUP], refs[1 + GROUP]
    outs, order = refs[GROUP + 2 : -1], refs[-1]
    sort_in(jumps, order)
    run(order, damp_ref[...][:, None], jnp.where(lax.axis_index("tm") < GROUP, 0.0, carry_ref[...]))
    sort_out(order, outs)


def finish_kernel(own_ref, *refs):
    pieces, out = refs[:GROUP], refs[GROUP]
    layers = out.shape[1]
    share = layers // GROUP
    first_slice = lax.axis_index("tm") == 0

    @pl.when(first_slice)
    def _():
        out[...] = own_ref[...]

    @pl.when(jnp.logical_not(first_slice))
    def _():
        near = near_side()
        for k, piece in enumerate(pieces):
            chunk = chunk_of(k)
            side = jnp.where(chunk < GROUP // 2, near, 1 - near)
            for j in range(share):
                slot = lax.rem(chunk, 2) * share + j
                layer = slot + side * (layers - 1 - 2 * slot)
                for c in range(3):
                    join_rows(out, (c, layer), [piece[j, c, odd] for odd in (0, 1)])


def shards(states, rate):
    slices = lax.axis_size("tm")
    slabs = lax.axis_size("gz")
    groups = slices // GROUP
    own = states[0]
    layers, rows, width = own.shape[1:]
    half, share = layers // 2, layers // GROUP
    tile = (3, 2, rows // 2, width)
    face = f32(3, STAGES, rows, width)
    piece = f32(share, *tile)
    team = lax.axis_index("tm") // GROUP

    def halo(value, pairs):
        return lax.ppermute(value, "gz", [(i, j % slabs) for i, j in pairs])

    def swap(parts):
        return [parts[0]] + [
            lax.ppermute(parts[k], "tm", [(i, i ^ partner(k)) for i in range(slices)])
            for k in range(1, GROUP)
        ]

    def onward(value, distance):
        flip = 2 * (distance % 2)
        pairs = [(i, ((i ^ flip) + distance * GROUP) % slices) for i in range(slices)]
        return lax.ppermute(value, "tm", pairs)

    far_face, near_face = call(faces_kernel, [face, face], own)
    near_face = halo(near_face, [(i, i ^ 1) for i in range(slabs)])
    far_face = halo(far_face, [(i, i + 1 if i % 2 else i - 1 + slabs) for i in range(slabs)])
    edges, middle, faded, damp = call(
        inside_kernel,
        [
            f32(STAGES, 2, 3, *tile),
            f32(2, half - STAGES, *tile),
            f32(2, STAGES, *tile),
            f32(share, *tile[1:]),
        ],
        own, rate,
        scratch=[pltpu.VMEM((2, half, *tile[1:]), jnp.float32)]
        + [pltpu.VMEM((layers, *tile), jnp.float32)] * 3,
        flops=1 << 26,
    )
    strip = pltpu.VMEM((STAGES + 1, STAGES, *tile), jnp.float32)
    near_jumps = call(
        near_kernel, f32(half, *tile), near_face, edges, middle, faded, scratch=[strip], flops=1 << 24
    )
    jumps = call(
        far_kernel, [piece] * GROUP, far_face, edges, middle, faded, near_jumps,
        scratch=[strip, pltpu.VMEM((2, half, *tile), jnp.float32)],
    )
    order = pltpu.VMEM((GROUP, *piece.shape), jnp.float32)
    jumps = swap(jumps)
    if groups > 1:
        total = call(total_kernel, piece, *jumps, damp, scratch=[order])
        carry = onward(total, 1)
        if groups > 2:
            carry = jnp.where(team < 1, 0.0, carry)
            fade, distance = damp[:, None] ** GROUP, 1
            while distance < groups - 1:
                carry = carry + jnp.where(team < distance, 0.0, fade * onward(carry, distance))
                distance, fade = 2 * distance, fade * fade
    else:
        carry = jnp.zeros(piece.shape, jnp.float32)
    news = call(spread_kernel, [piece] * GROUP, carry, *jumps, damp, scratch=[order])
    updated = call(finish_kernel, f32(*own.shape), own, *swap(news))
    return updated[None]


def solution(mesh):
    return jax.shard_map(
        shards,
        mesh=mesh,
        in_specs=(P("tm", None, "gz", None, None), P("gz", None, None)),
        out_specs=P("tm", None, "gz", None, None),
        check_vma=False,
    )
```

profile of v0, /device:TPU:0, one launch (start us, length us, event | category | flops | bytes accessed | tf_op | source)
XLA Modules:
  0.0 32.5 jit_solution(10526681645010918542)
XLA Ops:
  0.0 0.0 copy-start
  0.0 1.0 %copy-done = f32[1,3,16,16,128]{4,3,2,1,0:T(8,128)S(1)} copy-done((f32[1,3,16,16,128]{4,3,2,1,0:T(8,128)S(1)}, f32[1,3,16,16,128]{4,3,2,1,0:T(8,128)}, u32[]{:S(2)}) %copy-start) | copy-done | bytes 393240
  1.0 0.0 copy-start.2
  1.0 0.5 %collective-permute-start.1 = (f32[3,6,16,128]{3,2,1,0:T(8,128)S(1)}, f32[3,6,16,128]{3,2,1,0:T(8,128)S(1)}, u32[]{:S(2)}, u32[]{:S(2)}) collective-permute-start(f32[3,6,16,128]{3,2,1,0:T(8,128)S(1)} %get-tuple-element.23), channel_id=1, source_target_pairs={{0,1},{1,0},{2,3},{3,2},{4,5},{5,4},{6,7},{7,6},{8,9},{9,8},{10,11... | collective-permute-start | bytes 442376 | tf_op jit(solution)/shard_map/ppermute | solution.py:296
  1.5 2.6 %collective-permute-start = (f32[3,6,16,128]{3,2,1,0:T(8,128)S(1)}, f32[3,6,16,128]{3,2,1,0:T(8,128)S(1)}, u32[]{:S(2)}, u32[]{:S(2)}) collective-permute-start(f32[3,6,16,128]{3,2,1,0:T(8,128)S(1)} %get-tuple-element.19), channel_id=1, source_target_pairs={{0,3},{1,2},{2,1},{3,0},{4,7},{5,6},{6,5},{7,4},{8,11},{9,10},{10,... | collective-permute-start | bytes 442376 | tf_op jit(solution)/shard_map/ppermute | solution.py:296
  4.2 0.0 copy-done.2
  4.2 2.8 %shard_map.29 = (f32[6,2,3,3,2,8,128]{6,5,4,3,2,1,0:T(8,128)S(1)}, f32[2,2,3,2,8,128]{5,4,3,2,1,0:T(8,128)S(1)}, f32[2,6,3,2,8,128]{5,4,3,2,1,0:T(8,128)S(1)}, f32[4,2,8,128]{3,2,1,0:T(8,128)S(1)}) custom-call(f32[3,16,16,128]{3,2,1,0:T(8,128)S(1)} %bitcast.3, f32[16,16,128]{2,1,0:T(8,128)S(1)} %copy-done.2), custom_call_target="tpu_custom_call" | custom-call | flops 67108864 | bytes 1048576 | tf_op jit(solution)/shard_map/pallas_call | solution.py:24
  7.0 0.0 collective-permute-done.1.face_ref
  7.0 0.7 %shard_map.30.near_jumps = f32[8,3,2,8,128]{4,3,2,1,0:T(8,128)S(1)} custom-call(f32[3,6,16,128]{3,2,1,0:T(8,128)S(1)} %collective-permute-done.1.face_ref, f32[6,2,3,3,2,8,128]{6,5,4,3,2,1,0:T(8,128)S(1)} %get-tuple-element.20.edges, f32[2,2,3,2,8,128]{5,4,3,2,1,0:T(8,128)S(1)} %get-tuple-element.21.middle, f32[2,6,3,2,8,128]{5,4,3,2,1,0:T(8,128)S(1)} %get-tuple-element.22.faded), custom_call_target="tpu_custom_call" | custom-call | flops 16777216 | bytes 1048576 | tf_op jit(solution)/shard_map/pallas_call | solution.py:24
  7.7 0.6 %collective-permute-done.face_ref = f32[3,6,16,128]{3,2,1,0:T(8,128)S(1)} collective-permute-done((f32[3,6,16,128]{3,2,1,0:T(8,128)S(1)}, f32[3,6,16,128]{3,2,1,0:T(8,128)S(1)}, u32[]{:S(2)}, u32[]{:S(2)}) %collective-permute-start) | collective-permute-done | bytes 147488 | tf_op jit(solution)/shard_map/ppermute | solution.py:296
  8.3 0.7 %shard_map.31 = (f32[4,3,2,8,128]{4,3,2,1,0:T(8,128)S(1)}, f32[4,3,2,8,128]{4,3,2,1,0:T(8,128)S(1)}, f32[4,3,2,8,128]{4,3,2,1,0:T(8,128)S(1)}, f32[4,3,2,8,128]{4,3,2,1,0:T(8,128)S(1)}) custom-call(f32[3,6,16,128]{3,2,1,0:T(8,128)S(1)} %collective-permute-done.face_ref, f32[6,2,3,3,2,8,128]{6,5,4,3,2,1,0:T(8,128)S(1)} %get-tuple-element.20.edges, ...), custom_call_target="tpu_custom_call" | custom-call | tf_op jit(solution)/shard_map/pallas_call | solution.py:24
  9.0 2.4 %collective-permute-start.2 = (f32[4,3,2,8,128]{4,3,2,1,0:T(8,128)S(1)}, f32[4,3,2,8,128]{4,3,2,1,0:T(8,128)S(1)}, u32[]{:S(2)}, u32[]{:S(2)}) collective-permute-start(f32[4,3,2,8,128]{4,3,2,1,0:T(8,128)S(1)} %get-tuple-element.25), channel_id=1, source_target_pairs={{0,12},{4,8},{8,4},{12,0},{16,28},{20,24},{24,20},{28,16},{1,13},{... | collective-permute-start | bytes 294920 | tf_op jit(solution)/shard_map/ppermute | solution.py:300
  11.5 0.4 %collective-permute-start.3 = (f32[4,3,2,8,128]{4,3,2,1,0:T(8,128)S(1)}, f32[4,3,2,8,128]{4,3,2,1,0:T(8,128)S(1)}, u32[]{:S(2)}, u32[]{:S(2)}) collective-permute-start(f32[4,3,2,8,128]{4,3,2,1,0:T(8,128)S(1)} %get-tuple-element.26), channel_id=1, source_target_pairs={{0,8},{4,12},{8,0},{12,4},{16,24},{20,28},{24,16},{28,20},{1,9},{5... | collective-permute-start | bytes 294920 | tf_op jit(solution)/shard_map/ppermute | solution.py:300
  11.9 0.7 %collective-permute-start.4 = (f32[4,3,2,8,128]{4,3,2,1,0:T(8,128)S(1)}, f32[4,3,2,8,128]{4,3,2,1,0:T(8,128)S(1)}, u32[]{:S(2)}, u32[]{:S(2)}) collective-permute-start(f32[4,3,2,8,128]{4,3,2,1,0:T(8,128)S(1)} %get-tuple-element.27), channel_id=1, source_target_pairs={{0,4},{4,0},{8,12},{12,8},{16,20},{20,16},{24,28},{28,24},{1,5},{5... | collective-permute-start | bytes 294920 | tf_op jit(solution)/shard_map/ppermute | solution.py:300
  12.6 3.0 %collective-permute-done.2.refs_1_.refs_2_ = f32[4,3,2,8,128]{4,3,2,1,0:T(8,128)S(1)} collective-permute-done((f32[4,3,2,8,128]{4,3,2,1,0:T(8,128)S(1)}, f32[4,3,2,8,128]{4,3,2,1,0:T(8,128)S(1)}, u32[]{:S(2)}, u32[]{:S(2)}) %collective-permute-start.2) | collective-permute-done | bytes 98336 | tf_op jit(solution)/shard_map/ppermute | solution.py:300
  15.5 1.6 %collective-permute-done.3.refs_2_.refs_3_ = f32[4,3,2,8,128]{4,3,2,1,0:T(8,128)S(1)} collective-permute-done((f32[4,3,2,8,128]{4,3,2,1,0:T(8,128)S(1)}, f32[4,3,2,8,128]{4,3,2,1,0:T(8,128)S(1)}, u32[]{:S(2)}, u32[]{:S(2)}) %collective-permute-start.3) | collective-permute-done | bytes 98336 | tf_op jit(solution)/shard_map/ppermute | solution.py:300
  17.1 0.0 collective-permute-done.4.refs_3_.refs_4_
  17.2 0.1 shard_map.32
  17.2 0.0 copy-start.1
  17.2 3.7 %collective-permute-start.5 = (f32[4,3,2,8,128]{4,3,2,1,0:T(8,128)S(1)}, f32[4,3,2,8,128]{4,3,2,1,0:T(8,128)S(1)}, u32[]{:S(2)}, u32[]{:S(2)}) collective-permute-start(f32[4,3,2,8,128]{4,3,2,1,0:T(8,128)S(1)} %shard_map.32), channel_id=1, source_target_pairs={{0,24},{4,28},{8,16},{12,20},{16,8},{20,12},{24,0},{28,4},{1,25},{... | collective-permute-start | bytes 294920 | tf_op jit(solution)/shard_map/ppermute | solution.py:307
  20.9 2.9 %collective-permute-done.5.refs_0_ = f32[4,3,2,8,128]{4,3,2,1,0:T(8,128)S(1)} collective-permute-done((f32[4,3,2,8,128]{4,3,2,1,0:T(8,128)S(1)}, f32[4,3,2,8,128]{4,3,2,1,0:T(8,128)S(1)}, u32[]{:S(2)}, u32[]{:S(2)}) %collective-permute-start.5) | collective-permute-done | bytes 98336 | tf_op jit(solution)/shard_map/ppermute | solution.py:307
  23.8 0.1 shard_map.33
  23.9 2.9 %collective-permute-start.6 = (f32[4,3,2,8,128]{4,3,2,1,0:T(8,128)S(1)}, f32[4,3,2,8,128]{4,3,2,1,0:T(8,128)S(1)}, u32[]{:S(2)}, u32[]{:S(2)}) collective-permute-start(f32[4,3,2,8,128]{4,3,2,1,0:T(8,128)S(1)} %get-tuple-element.30), channel_id=1, source_target_pairs={{0,12},{4,8},{8,4},{12,0},{16,28},{20,24},{24,20},{28,16},{1,13},{... | collective-permute-start | bytes 294920 | tf_op jit(solution)/shard_map/ppermute | solution.py:300
  26.8 0.3 collective-permute-start.7
  27.1 0.4 %collective-permute-start.8 = (f32[4,3,2,8,128]{4,3,2,1,0:T(8,128)S(1)}, f32[4,3,2,8,128]{4,3,2,1,0:T(8,128)S(1)}, u32[]{:S(2)}, u32[]{:S(2)}) collective-permute-start(f32[4,3,2,8,128]{4,3,2,1,0:T(8,128)S(1)} %get-tuple-element.32), channel_id=1, source_target_pairs={{0,4},{4,0},{8,12},{12,8},{16,20},{20,16},{24,28},{28,24},{1,5},{5... | collective-permute-start | bytes 294920 | tf_op jit(solution)/shard_map/ppermute | solution.py:300
  27.4 2.6 %collective-permute-done.6.refs_1_ = f32[4,3,2,8,128]{4,3,2,1,0:T(8,128)S(1)} collective-permute-done((f32[4,3,2,8,128]{4,3,2,1,0:T(8,128)S(1)}, f32[4,3,2,8,128]{4,3,2,1,0:T(8,128)S(1)}, u32[]{:S(2)}, u32[]{:S(2)}) %collective-permute-start.6) | collective-permute-done | bytes 98336 | tf_op jit(solution)/shard_map/ppermute | solution.py:300
  30.1 1.4 %collective-permute-done.7.refs_2_ = f32[4,3,2,8,128]{4,3,2,1,0:T(8,128)S(1)} collective-permute-done((f32[4,3,2,8,128]{4,3,2,1,0:T(8,128)S(1)}, f32[4,3,2,8,128]{4,3,2,1,0:T(8,128)S(1)}, u32[]{:S(2)}, u32[]{:S(2)}) %collective-permute-start.7) | collective-permute-done | bytes 98336 | tf_op jit(solution)/shard_map/ppermute | solution.py:300
  31.4 0.3 collective-permute-done.8.refs_3_
  31.7 0.0 copy-done.1
  31.7 0.8 %shard_map.34 = f32[3,16,16,128]{3,2,1,0:T(8,128)} custom-call(f32[3,16,16,128]{3,2,1,0:T(8,128)S(1)} %bitcast.4, f32[4,3,2,8,128]{4,3,2,1,0:T(8,128)S(1)} %get-tuple-element.29.refs_0_, f32[4,3,2,8,128]{4,3,2,1,0:T(8,128)S(1)} %collective-permute-done.6.refs_1_, f32[4,3,2,8,128]{4,3,2,1,0:T(8,128)S(1)} %collective-permute-done.7.refs_2_, ...), custom_call_target="tpu_custom_call" | custom-call | tf_op jit(solution)/shard_map/pallas_call | solution.py:24
  (1 shorter events, 0.0 us)
Async XLA Ops:
  0.0 1.0 %copy-start = (f32[1,3,16,16,128]{4,3,2,1,0:T(8,128)S(1)}, f32[1,3,16,16,128]{4,3,2,1,0:T(8,128)}, u32[]{:S(2)}) copy-start(f32[1,3,16,16,128]{4,3,2,1,0:T(8,128)} %param.2) | copy-start | bytes 1179652
  1.0 3.2 %copy-start.2 = (f32[16,16,128]{2,1,0:T(8,128)S(1)}, f32[16,16,128]{2,1,0:T(8,128)}, u32[]{:S(2)}) copy-start(f32[16,16,128]{2,1,0:T(8,128)} %rate_ref.1) | copy-start | bytes 393220
  1.0 6.0 %collective-permute-start.1 = (f32[3,6,16,128]{3,2,1,0:T(8,128)S(1)}, f32[3,6,16,128]{3,2,1,0:T(8,128)S(1)}, u32[]{:S(2)}, u32[]{:S(2)}) collective-permute-start(f32[3,6,16,128]{3,2,1,0:T(8,128)S(1)} %get-tuple-element.23), channel_id=1, source_target_pairs={{0,1},{1,0},{2,3},{3,2},{4,5},{5,4},{6,7},{7,6},{8,9},{9,8},{10,11... | collective-permute-start | bytes 442376 | tf_op jit(solution)/shard_map/ppermute | solution.py:296
  1.5 6.8 %collective-permute-start = (f32[3,6,16,128]{3,2,1,0:T(8,128)S(1)}, f32[3,6,16,128]{3,2,1,0:T(8,128)S(1)}, u32[]{:S(2)}, u32[]{:S(2)}) collective-permute-start(f32[3,6,16,128]{3,2,1,0:T(8,128)S(1)} %get-tuple-element.19), channel_id=1, source_target_pairs={{0,3},{1,2},{2,1},{3,0},{4,7},{5,6},{6,5},{7,4},{8,11},{9,10},{10,... | collective-permute-start | bytes 442376 | tf_op jit(solution)/shard_map/ppermute | solution.py:296
  9.0 6.5 %collective-permute-start.2 = (f32[4,3,2,8,128]{4,3,2,1,0:T(8,128)S(1)}, f32[4,3,2,8,128]{4,3,2,1,0:T(8,128)S(1)}, u32[]{:S(2)}, u32[]{:S(2)}) collective-permute-start(f32[4,3,2,8,128]{4,3,2,1,0:T(8,128)S(1)} %get-tuple-element.25), channel_id=1, source_target_pairs={{0,12},{4,8},{8,4},{12,0},{16,28},{20,24},{24,20},{28,16},{1,13},{... | collective-permute-start | bytes 294920 | tf_op jit(solution)/shard_map/ppermute | solution.py:300
  11.5 5.7 %collective-permute-start.3 = (f32[4,3,2,8,128]{4,3,2,1,0:T(8,128)S(1)}, f32[4,3,2,8,128]{4,3,2,1,0:T(8,128)S(1)}, u32[]{:S(2)}, u32[]{:S(2)}) collective-permute-start(f32[4,3,2,8,128]{4,3,2,1,0:T(8,128)S(1)} %get-tuple-element.26), channel_id=1, source_target_pairs={{0,8},{4,12},{8,0},{12,4},{16,24},{20,28},{24,16},{28,20},{1,9},{5... | collective-permute-start | bytes 294920 | tf_op jit(solution)/shard_map/ppermute | solution.py:300
  11.9 5.2 %collective-permute-start.4 = (f32[4,3,2,8,128]{4,3,2,1,0:T(8,128)S(1)}, f32[4,3,2,8,128]{4,3,2,1,0:T(8,128)S(1)}, u32[]{:S(2)}, u32[]{:S(2)}) collective-permute-start(f32[4,3,2,8,128]{4,3,2,1,0:T(8,128)S(1)} %get-tuple-element.27), channel_id=1, source_target_pairs={{0,4},{4,0},{8,12},{12,8},{16,20},{20,16},{24,28},{28,24},{1,5},{5... | collective-permute-start | bytes 294920 | tf_op jit(solution)/shard_map/ppermute | solution.py:300
  17.2 14.5 %copy-start.1 = (f32[1,3,16,16,128]{4,3,2,1,0:T(8,128)S(1)}, f32[1,3,16,16,128]{4,3,2,1,0:T(8,128)}, u32[]{:S(2)}) copy-start(f32[1,3,16,16,128]{4,3,2,1,0:T(8,128)} %param.2) | copy-start | bytes 1179652
  17.2 6.5 %collective-permute-start.5 = (f32[4,3,2,8,128]{4,3,2,1,0:T(8,128)S(1)}, f32[4,3,2,8,128]{4,3,2,1,0:T(8,128)S(1)}, u32[]{:S(2)}, u32[]{:S(2)}) collective-permute-start(f32[4,3,2,8,128]{4,3,2,1,0:T(8,128)S(1)} %shard_map.32), channel_id=1, source_target_pairs={{0,24},{4,28},{8,16},{12,20},{16,8},{20,12},{24,0},{28,4},{1,25},{... | collective-permute-start | bytes 294920 | tf_op jit(solution)/shard_map/ppermute | solution.py:307
  23.9 6.2 %collective-permute-start.6 = (f32[4,3,2,8,128]{4,3,2,1,0:T(8,128)S(1)}, f32[4,3,2,8,128]{4,3,2,1,0:T(8,128)S(1)}, u32[]{:S(2)}, u32[]{:S(2)}) collective-permute-start(f32[4,3,2,8,128]{4,3,2,1,0:T(8,128)S(1)} %get-tuple-element.30), channel_id=1, source_target_pairs={{0,12},{4,8},{8,4},{12,0},{16,28},{20,24},{24,20},{28,16},{1,13},{... | collective-permute-start | bytes 294920 | tf_op jit(solution)/shard_map/ppermute | solution.py:300
  26.8 4.7 %collective-permute-start.7 = (f32[4,3,2,8,128]{4,3,2,1,0:T(8,128)S(1)}, f32[4,3,2,8,128]{4,3,2,1,0:T(8,128)S(1)}, u32[]{:S(2)}, u32[]{:S(2)}) collective-permute-start(f32[4,3,2,8,128]{4,3,2,1,0:T(8,128)S(1)} %get-tuple-element.31), channel_id=1, source_target_pairs={{0,8},{4,12},{8,0},{12,4},{16,24},{20,28},{24,16},{28,20},{1,9},{5... | collective-permute-start | bytes 294920 | tf_op jit(solution)/shard_map/ppermute | solution.py:300
  27.1 4.6 %collective-permute-start.8 = (f32[4,3,2,8,128]{4,3,2,1,0:T(8,128)S(1)}, f32[4,3,2,8,128]{4,3,2,1,0:T(8,128)S(1)}, u32[]{:S(2)}, u32[]{:S(2)}) collective-permute-start(f32[4,3,2,8,128]{4,3,2,1,0:T(8,128)S(1)} %get-tuple-element.32), channel_id=1, source_target_pairs={{0,4},{4,0},{8,12},{12,8},{16,20},{20,16},{24,28},{28,24},{1,5},{5... | collective-permute-start | bytes 294920 | tf_op jit(solution)/shard_map/ppermute | solution.py:300
where the time goes:
time: 32.6 us; the launch traced here: 32.5 us
  starting transfers between devices  13.9 us (43%)
  waiting for transfers between devices  12.3 us (38%)
  Pallas kernels  5.2 us (16%)
  local copies, waits for them, and re-layouts  1.01 us (3%)
    ppermute x6, waiting for transfers between devices, swap(): lax.ppermute(parts[k], 'tm', [(i, i ^ partner(k)) for i in range(slices)])  8.82 us
    ppermute x6, starting transfers between devices, swap(): lax.ppermute(parts[k], 'tm', [(i, i ^ partner(k)) for i in range(slices)])  7.11 us
    pallas_call x7, Pallas kernels, call(): pl.pallas_call(kernel, out_shape=out_shape, in_specs=[VMEM] * len(args),...  5.2 us
    ppermute x1, starting transfers between devices, onward(): return lax.ppermute(value, 'tm', pairs)  3.67 us
    ppermute x2, starting transfers between devices, halo(): return lax.ppermute(value, 'gz', [(i, j % slabs) for i, j in pairs])  3.16 us
    ppermute x1, waiting for transfers between devices, onward(): return lax.ppermute(value, 'tm', pairs)  2.87 us
    unnamed x6, local copies, waits for them, and re-layouts  1.01 us
  transfers between devices with their start and end apart: 9, of which 7 were waited for; matrix products, arithmetic and copies ran while one was open for 0% of the time, Pallas kernels for 11%

commit v1 on v0

--- a/solution.py
+++ b/solution.py
@@ -104,12 +104,16 @@
     return [[new[c][odd] + beta * base[c][odd] for odd in (0, 1)] for c in range(3)]
 
 
-def faces_kernel(own_ref, far_ref, near_ref):
-    layers, width = own_ref.shape[1], near_ref.shape[1]
+def faces_kernel(own_ref, *refs):
+    *far_refs, near_ref = refs
+    layers, width, part = own_ref.shape[1], near_ref.shape[1], far_refs[0].shape[1]
     near = near_side()
+    far = 1 - near
     top = layers - width
-    far_ref[...] = own_ref[:, pl.ds((1 - near) * top, width)]
     near_ref[...] = own_ref[:, pl.ds(near * top, width)]
+    for j, far_ref in enumerate(far_refs):
+        start = far * (top + j * part) + (1 - far) * (width - (j + 1) * part)
+        far_ref[...] = own_ref[:, pl.ds(start, part)]
 
 
 def inside_kernel(own_ref, rate_ref, edges, middle, faded, damp_ref, damps, *fields):
@@ -118,71 +122,63 @@
     slices = lax.axis_size("tm")
     keep = (lax.axis_index("tm") != 0).astype(jnp.float32)
 
-    def fill(z, _):
-        for c in range(3):
-            for odd, value in enumerate(split_rows(own_ref, c, z)):
-                fields[0][z, c, odd] = value
-        return 0
-
-    lax.fori_loop(0, layers, fill, 0, unroll=2)
-
-    def save(stage, field):
-        for j in range(3):
-            store(edges, (stage, 0, j), load(field, stage + j))
-            store(edges, (stage, 1, j), load(field, layers - 1 - stage - j))
-
-    def sweep(stage, source, target, base, alpha, beta):
-        def body(turn, carry):
-            below, here = carry
-            for k in range(2):
-                z = stage + 2 * turn + k
-                above = load(source, z + 1)
-                new = advance(below, here, above, alpha)
-                if beta is not None:
-                    new = blend(new, beta, load(base, z))
-                store(target, (z,), new)
-                below, here = here, above
-            return below, here
-
-        first = (load(source, stage - 1), load(source, stage))
-        lax.fori_loop(0, (layers - 2 * stage) // 2, body, first)
-
-    save(0, fields[0])
-    for stage in range(1, STAGES + 1):
-        kind = (stage - 1) % 3
-        target = fields[(kind + 1) % 3]
-        sweep(stage, fields[kind], target, fields[0], *MIX[kind])
-        if stage < STAGES:
-            save(stage, target)
+    def save(stage, z, value):
+        low, high = z - stage, layers - 1 - stage - z
+        if low < 3:
+            store(edges, (stage, 0, low), value)
+        if high < 3:
+            store(edges, (stage, 1, high), value)
 
     for z in range(layers):
         side, slot = (0, z) if z < half else (1, layers - 1 - z)
         damp = [jnp.exp(r * (-1.0 / slices)) for r in split_rows(rate_ref, z)]
+        start = [split_rows(own_ref, c, z) for c in range(3)]
+        store(fields[0], (z,), start)
+        save(0, z, start)
         for odd in (0, 1):
             damps[side, slot, odd] = damp[odd]
-        for c in range(3):
-            start = split_rows(own_ref, c, z)
-            for odd in (0, 1):
-                lost = damp[odd] * keep * start[odd]
-                if slot < STAGES:
-                    faded[side, slot, c, odd] = lost
-                else:
-                    middle[side, slot - STAGES, c, odd] = fields[0][z, c, odd] - lost
-
+        lost = [[damp[odd] * keep * start[c][odd] for odd in (0, 1)] for c in range(3)]
+        if slot < STAGES:
+            store(faded, (side, slot), lost)
+        else:
+            store(middle, (side, slot - STAGES), lost)
+
+    for stage in range(1, STAGES + 1):
+        kind = (stage - 1) % 3
+        alpha, beta = MIX[kind]
+        source, target = fields[kind], fields[(kind + 1) % 3]
+        below, here = load(source, stage - 1), load(source, stage)
+        for z in range(stage, layers - stage):
+            above = load(source, z + 1)
+            new = advance(below, here, above, alpha)
+            if beta is not None:
+                new = blend(new, beta, load(fields[0], z))
+            if stage < STAGES:
+                store(target, (z,), new)
+                save(stage, z, new)
+            else:
+                side, slot = (0, z) if z < half else (1, layers - 1 - z)
+                lost = load(middle, side, slot - STAGES)
+                store(
+                    middle,
+                    (side, slot - STAGES),
+                    [[new[c][odd] - lost[c][odd] for odd in (0, 1)] for c in range(3)],
+                )
+            below, here = here, above
+
+    chunk, near = chunk_of(0), near_side()
     share = layers // GROUP
-    chunk, near = chunk_of(0), near_side()
     side = jnp.where(chunk < GROUP // 2, near, 1 - near)
     damp_ref[...] = damps[side, pl.ds(lax.rem(chunk, 2) * share, share)]
 
 
-def border(side, face_ref, edges, middle, faded, jumps, strip):
+def border(side, faces, edges, middle, faded, jumps, strip):
     width = STAGES
     upward = 1.0 - 2.0 * side.astype(jnp.float32)
+    part = faces[0].shape[1]
     for slot in range(width):
-        layer = slot + side * (width - 1 - 2 * slot)
-        for c in range(3):
-            for odd, value in enumerate(split_rows(face_ref, c, layer)):
-                strip[0, slot, c, odd] = value
+        layer = slot % part + side * (part - 1 - 2 * (slot % part))
+        store(strip, (0, slot), [split_rows(faces[slot // part], c, layer) for c in range(3)])
 
     def at(stage, slot):
         if slot < width:
@@ -212,12 +208,12 @@
 
 
 def near_kernel(face_ref, edges, middle, faded, jumps, strip):
-    border(near_side(), face_ref, edges, middle, faded, jumps, strip)
-
-
-def far_kernel(face_ref, edges, middle, faded, near_jumps, *refs):
+    border(near_side(), [face_ref], edges, middle, faded, jumps, strip)
+
+
+def far_kernel(outer_ref, inner_ref, edges, middle, faded, near_jumps, *refs):
     outs, strip, jumps = refs[:GROUP], refs[GROUP], refs[GROUP + 1]
-    border(1 - near_side(), face_ref, edges, middle, faded, jumps.at[1], strip)
+    border(1 - near_side(), [outer_ref, inner_ref], edges, middle, faded, jumps.at[1], strip)
     jumps[0] = near_jumps[...]
     share = outs[0].shape[0]
     for k, out in enumerate(outs):
@@ -288,7 +284,7 @@
     layers, rows, width = own.shape[1:]
     half, share = layers // 2, layers // GROUP
     tile = (3, 2, rows // 2, width)
-    face = f32(3, STAGES, rows, width)
+    face, part = f32(3, STAGES, rows, width), f32(3, STAGES // 2, rows, width)
     piece = f32(share, *tile)
     team = lax.axis_index("tm") // GROUP
 
@@ -306,9 +302,12 @@
         pairs = [(i, ((i ^ flip) + distance * GROUP) % slices) for i in range(slices)]
         return lax.ppermute(value, "tm", pairs)
 
-    far_face, near_face = call(faces_kernel, [face, face], own)
+    *far_faces, near_face = call(faces_kernel, [part, part, face], own)
     near_face = halo(near_face, [(i, i ^ 1) for i in range(slabs)])
-    far_face = halo(far_face, [(i, i + 1 if i % 2 else i - 1 + slabs) for i in range(slabs)])
+    far_faces = [
+        halo(face, [(i, i + 1 if i % 2 else i - 1 + slabs) for i in range(slabs)])
+        for face in far_faces
+    ]
     edges, middle, faded, damp = call(
         inside_kernel,
         [
@@ -327,7 +326,7 @@
         near_kernel, f32(half, *tile), near_face, edges, middle, faded, scratch=[strip], flops=1 << 24
     )
     jumps = call(
-        far_kernel, [piece] * GROUP, far_face, edges, middle, faded, near_jumps,
+        far_kernel, [piece] * GROUP, *far_faces, edges, middle, faded, near_jumps,
         scratch=[strip, pltpu.VMEM((2, half, *tile), jnp.float32)],
     )
     order = pltpu.VMEM((GROUP, *piece.shape), jnp.float32)

time: 32.6 us -> 32.4 us (level)
  Pallas kernels: 5.2 us -> 3.24 us
  waiting for transfers between devices: 12.3 us -> 14 us
    ppermute x2 -> x3, waiting for transfers between devices: 0.6 us -> 2.74 us  [halo(): return lax.ppermute(value, 'gz', [(i, j % slabs) for i, j in pairs])]
    pallas_call x7, Pallas kernels: 5.2 us -> 3.24 us  [call(): pl.pallas_call(kernel, out_shape=out_shape, in_specs=[VMEM] * len(args),...]
    ppermute x6, waiting for transfers between devices: 8.82 us -> 8.44 us  [swap(): lax.ppermute(parts[k], 'tm', [(i, i ^ partner(k)) for i in range(slices)])]
    ppermute x2 -> x3, starting transfers between devices: 3.16 us -> 3.18 us  [halo(): return lax.ppermute(value, 'gz', [(i, j % slabs) for i, j in pairs])]
  transfers between devices with their start and end apart: 9 -> 10, of which waited for: 7 -> 8; matrix products, arithmetic and copies ran while one was open for 0% -> 0% of each run, Pallas kernels for 11% -> 5%
where the time goes in v1:
time: 32.4 us; the launch traced here: 32.3 us
  starting transfers between devices  14 us (43%)
  waiting for transfers between devices  14 us (43%)
  Pallas kernels  3.24 us (10%)
  local copies, waits for them, and re-layouts  1.01 us (3%)
    ppermute x6, waiting for transfers between devices, swap(): lax.ppermute(parts[k], 'tm', [(i, i ^ partner(k)) for i in range(slices)])  8.44 us
    ppermute x6, starting transfers between devices, swap(): lax.ppermute(parts[k], 'tm', [(i, i ^ partner(k)) for i in range(slices)])  7.11 us
    ppermute x1, starting transfers between devices, onward(): return lax.ppermute(value, 'tm', pairs)  3.7 us
    pallas_call x7, Pallas kernels, call(): pl.pallas_call(kernel, out_shape=out_shape, in_specs=[VMEM] * len(args),...  3.24 us
    ppermute x3, starting transfers between devices, halo(): return lax.ppermute(value, 'gz', [(i, j % slabs) for i, j in pairs])  3.18 us
    ppermute x1, waiting for transfers between devices, onward(): return lax.ppermute(value, 'tm', pairs)  2.84 us
    ppermute x3, waiting for transfers between devices, halo(): return lax.ppermute(value, 'gz', [(i, j % slabs) for i, j in pairs])  2.74 us
    unnamed x6, local copies, waits for them, and re-layouts  1.01 us
  transfers between devices with their start and end apart: 10, of which 8 were waited for; matrix products, arithmetic and copies ran while one was open for 0% of the time, Pallas kernels for 5%

profile of v1, /device:TPU:0, one launch (start us, length us, event | category | flops | bytes accessed | tf_op | source)
XLA Modules:
  0.0 32.3 jit_solution(17382387425465162888)
XLA Ops:
  0.0 0.0 copy-start
  0.0 1.0 %copy-done = f32[1,3,16,16,128]{4,3,2,1,0:T(8,128)S(1)} copy-done((f32[1,3,16,16,128]{4,3,2,1,0:T(8,128)S(1)}, f32[1,3,16,16,128]{4,3,2,1,0:T(8,128)}, u32[]{:S(2)}) %copy-start) | copy-done | bytes 393240
  1.0 0.0 copy-start.2
  1.0 0.5 %collective-permute-start.2 = (f32[3,6,16,128]{3,2,1,0:T(8,128)S(1)}, f32[3,6,16,128]{3,2,1,0:T(8,128)S(1)}, u32[]{:S(2)}, u32[]{:S(2)}) collective-permute-start(f32[3,6,16,128]{3,2,1,0:T(8,128)S(1)} %get-tuple-element.25), channel_id=1, source_target_pairs={{0,1},{1,0},{2,3},{3,2},{4,5},{5,4},{6,7},{7,6},{8,9},{9,8},{10,11... | collective-permute-start | bytes 442376 | tf_op jit(solution)/shard_map/ppermute | solution.py:292
  1.5 2.6 %collective-permute-start = (f32[3,3,16,128]{3,2,1,0:T(8,128)S(1)}, f32[3,3,16,128]{3,2,1,0:T(8,128)S(1)}, u32[]{:S(2)}, u32[]{:S(2)}) collective-permute-start(f32[3,3,16,128]{3,2,1,0:T(8,128)S(1)} %get-tuple-element.20), channel_id=1, source_target_pairs={{0,3},{1,2},{2,1},{3,0},{4,7},{5,6},{6,5},{7,4},{8,11},{9,10},{10,... | collective-permute-start | bytes 221192 | tf_op jit(solution)/shard_map/ppermute | solution.py:292
  4.2 0.0 collective-permute-start.1
  4.2 0.0 copy-done.2
  4.2 0.8 %shard_map.29 = (f32[6,2,3,3,2,8,128]{6,5,4,3,2,1,0:T(8,128)S(1)}, f32[2,2,3,2,8,128]{5,4,3,2,1,0:T(8,128)S(1)}, f32[2,6,3,2,8,128]{5,4,3,2,1,0:T(8,128)S(1)}, f32[4,2,8,128]{3,2,1,0:T(8,128)S(1)}) custom-call(f32[3,16,16,128]{3,2,1,0:T(8,128)S(1)} %bitcast.3, f32[16,16,128]{2,1,0:T(8,128)S(1)} %copy-done.2), custom_call_target="tpu_custom_call" | custom-call | flops 67108864 | bytes 1048576 | tf_op jit(solution)/shard_map/pallas_call | solution.py:24
  5.1 0.0 collective-permute-done.2.face_ref
  5.1 0.7 %shard_map.30.near_jumps = f32[8,3,2,8,128]{4,3,2,1,0:T(8,128)S(1)} custom-call(f32[3,6,16,128]{3,2,1,0:T(8,128)S(1)} %collective-permute-done.2.face_ref, f32[6,2,3,3,2,8,128]{6,5,4,3,2,1,0:T(8,128)S(1)} %get-tuple-element.22.edges, f32[2,2,3,2,8,128]{5,4,3,2,1,0:T(8,128)S(1)} %get-tuple-element.23.middle, f32[2,6,3,2,8,128]{5,4,3,2,1,0:T(8,128)S(1)} %get-tuple-element.24.faded), custom_call_target="tpu_custom_call" | custom-call | flops 16777216 | bytes 1048576 | tf_op jit(solution)/shard_map/pallas_call | solution.py:24
  5.8 1.0 %collective-permute-done.outer_ref = f32[3,3,16,128]{3,2,1,0:T(8,128)S(1)} collective-permute-done((f32[3,3,16,128]{3,2,1,0:T(8,128)S(1)}, f32[3,3,16,128]{3,2,1,0:T(8,128)S(1)}, u32[]{:S(2)}, u32[]{:S(2)}) %collective-permute-start) | collective-permute-done | bytes 73760 | tf_op jit(solution)/shard_map/ppermute | solution.py:292
  6.8 1.7 %collective-permute-done.1.inner_ref = f32[3,3,16,128]{3,2,1,0:T(8,128)S(1)} collective-permute-done((f32[3,3,16,128]{3,2,1,0:T(8,128)S(1)}, f32[3,3,16,128]{3,2,1,0:T(8,128)S(1)}, u32[]{:S(2)}, u32[]{:S(2)}) %collective-permute-start.1) | collective-permute-done | bytes 73760 | tf_op jit(solution)/shard_map/ppermute | solution.py:292
  8.5 0.7 %shard_map.31 = (f32[4,3,2,8,128]{4,3,2,1,0:T(8,128)S(1)}, f32[4,3,2,8,128]{4,3,2,1,0:T(8,128)S(1)}, f32[4,3,2,8,128]{4,3,2,1,0:T(8,128)S(1)}, f32[4,3,2,8,128]{4,3,2,1,0:T(8,128)S(1)}) custom-call(f32[3,3,16,128]{3,2,1,0:T(8,128)S(1)} %collective-permute-done.outer_ref, f32[3,3,16,128]{3,2,1,0:T(8,128)S(1)} %collective-permute-done.1.inner_ref, ...), custom_call_target="tpu_custom_call" | custom-call | tf_op jit(solution)/shard_map/pallas_call | solution.py:24
  9.2 2.6 %collective-permute-start.3 = (f32[4,3,2,8,128]{4,3,2,1,0:T(8,128)S(1)}, f32[4,3,2,8,128]{4,3,2,1,0:T(8,128)S(1)}, u32[]{:S(2)}, u32[]{:S(2)}) collective-permute-start(f32[4,3,2,8,128]{4,3,2,1,0:T(8,128)S(1)} %get-tuple-element.27), channel_id=1, source_target_pairs={{0,12},{4,8},{8,4},{12,0},{16,28},{20,24},{24,20},{28,16},{1,13},{... | collective-permute-start | bytes 294920 | tf_op jit(solution)/shard_map/ppermute | solution.py:296
  11.8 0.4 %collective-permute-start.4 = (f32[4,3,2,8,128]{4,3,2,1,0:T(8,128)S(1)}, f32[4,3,2,8,128]{4,3,2,1,0:T(8,128)S(1)}, u32[]{:S(2)}, u32[]{:S(2)}) collective-permute-start(f32[4,3,2,8,128]{4,3,2,1,0:T(8,128)S(1)} %get-tuple-element.28), channel_id=1, source_target_pairs={{0,8},{4,12},{8,0},{12,4},{16,24},{20,28},{24,16},{28,20},{1,9},{5... | collective-permute-start | bytes 294920 | tf_op jit(solution)/shard_map/ppermute | solution.py:296
  12.3 0.5 %collective-permute-start.5 = (f32[4,3,2,8,128]{4,3,2,1,0:T(8,128)S(1)}, f32[4,3,2,8,128]{4,3,2,1,0:T(8,128)S(1)}, u32[]{:S(2)}, u32[]{:S(2)}) collective-permute-start(f32[4,3,2,8,128]{4,3,2,1,0:T(8,128)S(1)} %get-tuple-element.29), channel_id=1, source_target_pairs={{0,4},{4,0},{8,12},{12,8},{16,20},{20,16},{24,28},{28,24},{1,5},{5... | collective-permute-start | bytes 294920 | tf_op jit(solution)/shard_map/ppermute | solution.py:296
  12.8 3.0 %collective-permute-done.3.refs_1_.refs_2_ = f32[4,3,2,8,128]{4,3,2,1,0:T(8,128)S(1)} collective-permute-done((f32[4,3,2,8,128]{4,3,2,1,0:T(8,128)S(1)}, f32[4,3,2,8,128]{4,3,2,1,0:T(8,128)S(1)}, u32[]{:S(2)}, u32[]{:S(2)}) %collective-permute-start.3) | collective-permute-done | bytes 98336 | tf_op jit(solution)/shard_map/ppermute | solution.py:296
  15.8 1.4 %collective-permute-done.4.refs_2_.refs_3_ = f32[4,3,2,8,128]{4,3,2,1,0:T(8,128)S(1)} collective-permute-done((f32[4,3,2,8,128]{4,3,2,1,0:T(8,128)S(1)}, f32[4,3,2,8,128]{4,3,2,1,0:T(8,128)S(1)}, u32[]{:S(2)}, u32[]{:S(2)}) %collective-permute-start.4) | collective-permute-done | bytes 98336 | tf_op jit(solution)/shard_map/ppermute | solution.py:296
  17.2 0.0 collective-permute-done.5.refs_3_.refs_4_
  17.2 0.1 shard_map.32
  17.3 0.0 copy-start.1
  17.3 3.7 %collective-permute-start.6 = (f32[4,3,2,8,128]{4,3,2,1,0:T(8,128)S(1)}, f32[4,3,2,8,128]{4,3,2,1,0:T(8,128)S(1)}, u32[]{:S(2)}, u32[]{:S(2)}) collective-permute-start(f32[4,3,2,8,128]{4,3,2,1,0:T(8,128)S(1)} %shard_map.32), channel_id=1, source_target_pairs={{0,24},{4,28},{8,16},{12,20},{16,8},{20,12},{24,0},{28,4},{1,25},{... | collective-permute-start | bytes 294920 | tf_op jit(solution)/shard_map/ppermute | solution.py:303
  21.0 2.8 %collective-permute-done.6.refs_0_ = f32[4,3,2,8,128]{4,3,2,1,0:T(8,128)S(1)} collective-permute-done((f32[4,3,2,8,128]{4,3,2,1,0:T(8,128)S(1)}, f32[4,3,2,8,128]{4,3,2,1,0:T(8,128)S(1)}, u32[]{:S(2)}, u32[]{:S(2)}) %collective-permute-start.6) | collective-permute-done | bytes 98336 | tf_op jit(solution)/shard_map/ppermute | solution.py:303
  23.9 0.1 shard_map.33
  24.0 2.6 %collective-permute-start.7 = (f32[4,3,2,8,128]{4,3,2,1,0:T(8,128)S(1)}, f32[4,3,2,8,128]{4,3,2,1,0:T(8,128)S(1)}, u32[]{:S(2)}, u32[]{:S(2)}) collective-permute-start(f32[4,3,2,8,128]{4,3,2,1,0:T(8,128)S(1)} %get-tuple-element.32), channel_id=1, source_target_pairs={{0,12},{4,8},{8,4},{12,0},{16,28},{20,24},{24,20},{28,16},{1,13},{... | collective-permute-start | bytes 294920 | tf_op jit(solution)/shard_map/ppermute | solution.py:296
  26.6 0.3 %collective-permute-start.8 = (f32[4,3,2,8,128]{4,3,2,1,0:T(8,128)S(1)}, f32[4,3,2,8,128]{4,3,2,1,0:T(8,128)S(1)}, u32[]{:S(2)}, u32[]{:S(2)}) collective-permute-start(f32[4,3,2,8,128]{4,3,2,1,0:T(8,128)S(1)} %get-tuple-element.33), channel_id=1, source_target_pairs={{0,8},{4,12},{8,0},{12,4},{16,24},{20,28},{24,16},{28,20},{1,9},{5... | collective-permute-start | bytes 294920 | tf_op jit(solution)/shard_map/ppermute | solution.py:296
  26.9 0.6 %collective-permute-start.9 = (f32[4,3,2,8,128]{4,3,2,1,0:T(8,128)S(1)}, f32[4,3,2,8,128]{4,3,2,1,0:T(8,128)S(1)}, u32[]{:S(2)}, u32[]{:S(2)}) collective-permute-start(f32[4,3,2,8,128]{4,3,2,1,0:T(8,128)S(1)} %get-tuple-element.34), channel_id=1, source_target_pairs={{0,4},{4,0},{8,12},{12,8},{16,20},{20,16},{24,28},{28,24},{1,5},{5... | collective-permute-start | bytes 294920 | tf_op jit(solution)/shard_map/ppermute | solution.py:296
  27.5 2.3 %collective-permute-done.7.refs_1_ = f32[4,3,2,8,128]{4,3,2,1,0:T(8,128)S(1)} collective-permute-done((f32[4,3,2,8,128]{4,3,2,1,0:T(8,128)S(1)}, f32[4,3,2,8,128]{4,3,2,1,0:T(8,128)S(1)}, u32[]{:S(2)}, u32[]{:S(2)}) %collective-permute-start.7) | collective-permute-done | bytes 98336 | tf_op jit(solution)/shard_map/ppermute | solution.py:296
  29.8 1.4 %collective-permute-done.8.refs_2_ = f32[4,3,2,8,128]{4,3,2,1,0:T(8,128)S(1)} collective-permute-done((f32[4,3,2,8,128]{4,3,2,1,0:T(8,128)S(1)}, f32[4,3,2,8,128]{4,3,2,1,0:T(8,128)S(1)}, u32[]{:S(2)}, u32[]{:S(2)}) %collective-permute-start.8) | collective-permute-done | bytes 98336 | tf_op jit(solution)/shard_map/ppermute | solution.py:296
  31.2 0.3 %collective-permute-done.9.refs_3_ = f32[4,3,2,8,128]{4,3,2,1,0:T(8,128)S(1)} collective-permute-done((f32[4,3,2,8,128]{4,3,2,1,0:T(8,128)S(1)}, f32[4,3,2,8,128]{4,3,2,1,0:T(8,128)S(1)}, u32[]{:S(2)}, u32[]{:S(2)}) %collective-permute-start.9) | collective-permute-done | bytes 98336 | tf_op jit(solution)/shard_map/ppermute | solution.py:296
  31.5 0.0 copy-done.1
  31.5 0.8 %shard_map.34 = f32[3,16,16,128]{3,2,1,0:T(8,128)} custom-call(f32[3,16,16,128]{3,2,1,0:T(8,128)S(1)} %bitcast.4, f32[4,3,2,8,128]{4,3,2,1,0:T(8,128)S(1)} %get-tuple-element.31.refs_0_, f32[4,3,2,8,128]{4,3,2,1,0:T(8,128)S(1)} %collective-permute-done.7.refs_1_, f32[4,3,2,8,128]{4,3,2,1,0:T(8,128)S(1)} %collective-permute-done.8.refs_2_, ...), custom_call_target="tpu_custom_call" | custom-call | tf_op jit(solution)/shard_map/pallas_call | solution.py:24
  (1 shorter events, 0.0 us)
Async XLA Ops:
  0.0 1.0 %copy-start = (f32[1,3,16,16,128]{4,3,2,1,0:T(8,128)S(1)}, f32[1,3,16,16,128]{4,3,2,1,0:T(8,128)}, u32[]{:S(2)}) copy-start(f32[1,3,16,16,128]{4,3,2,1,0:T(8,128)} %param.2) | copy-start | bytes 1179652
  1.0 3.2 %copy-start.2 = (f32[16,16,128]{2,1,0:T(8,128)S(1)}, f32[16,16,128]{2,1,0:T(8,128)}, u32[]{:S(2)}) copy-start(f32[16,16,128]{2,1,0:T(8,128)} %rate_ref.1) | copy-start | bytes 393220
  1.0 4.0 %collective-permute-start.2 = (f32[3,6,16,128]{3,2,1,0:T(8,128)S(1)}, f32[3,6,16,128]{3,2,1,0:T(8,128)S(1)}, u32[]{:S(2)}, u32[]{:S(2)}) collective-permute-start(f32[3,6,16,128]{3,2,1,0:T(8,128)S(1)} %get-tuple-element.25), channel_id=1, source_target_pairs={{0,1},{1,0},{2,3},{3,2},{4,5},{5,4},{6,7},{7,6},{8,9},{9,8},{10,11... | collective-permute-start | bytes 442376 | tf_op jit(solution)/shard_map/ppermute | solution.py:292
  1.5 5.2 %collective-permute-start = (f32[3,3,16,128]{3,2,1,0:T(8,128)S(1)}, f32[3,3,16,128]{3,2,1,0:T(8,128)S(1)}, u32[]{:S(2)}, u32[]{:S(2)}) collective-permute-start(f32[3,3,16,128]{3,2,1,0:T(8,128)S(1)} %get-tuple-element.20), channel_id=1, source_target_pairs={{0,3},{1,2},{2,1},{3,0},{4,7},{5,6},{6,5},{7,4},{8,11},{9,10},{10,... | collective-permute-start | bytes 221192 | tf_op jit(solution)/shard_map/ppermute | solution.py:292
  4.2 4.3 %collective-permute-start.1 = (f32[3,3,16,128]{3,2,1,0:T(8,128)S(1)}, f32[3,3,16,128]{3,2,1,0:T(8,128)S(1)}, u32[]{:S(2)}, u32[]{:S(2)}) collective-permute-start(f32[3,3,16,128]{3,2,1,0:T(8,128)S(1)} %get-tuple-element.21), channel_id=1, source_target_pairs={{0,3},{1,2},{2,1},{3,0},{4,7},{5,6},{6,5},{7,4},{8,11},{9,10},{10,... | collective-permute-start | bytes 221192 | tf_op jit(solution)/shard_map/ppermute | solution.py:292
  9.2 6.6 %collective-permute-start.3 = (f32[4,3,2,8,128]{4,3,2,1,0:T(8,128)S(1)}, f32[4,3,2,8,128]{4,3,2,1,0:T(8,128)S(1)}, u32[]{:S(2)}, u32[]{:S(2)}) collective-permute-start(f32[4,3,2,8,128]{4,3,2,1,0:T(8,128)S(1)} %get-tuple-element.27), channel_id=1, source_target_pairs={{0,12},{4,8},{8,4},{12,0},{16,28},{20,24},{24,20},{28,16},{1,13},{... | collective-permute-start | bytes 294920 | tf_op jit(solution)/shard_map/ppermute | solution.py:296
  11.8 5.4 %collective-permute-start.4 = (f32[4,3,2,8,128]{4,3,2,1,0:T(8,128)S(1)}, f32[4,3,2,8,128]{4,3,2,1,0:T(8,128)S(1)}, u32[]{:S(2)}, u32[]{:S(2)}) collective-permute-start(f32[4,3,2,8,128]{4,3,2,1,0:T(8,128)S(1)} %get-tuple-element.28), channel_id=1, source_target_pairs={{0,8},{4,12},{8,0},{12,4},{16,24},{20,28},{24,16},{28,20},{1,9},{5... | collective-permute-start | bytes 294920 | tf_op jit(solution)/shard_map/ppermute | solution.py:296
  12.3 5.0 %collective-permute-start.5 = (f32[4,3,2,8,128]{4,3,2,1,0:T(8,128)S(1)}, f32[4,3,2,8,128]{4,3,2,1,0:T(8,128)S(1)}, u32[]{:S(2)}, u32[]{:S(2)}) collective-permute-start(f32[4,3,2,8,128]{4,3,2,1,0:T(8,128)S(1)} %get-tuple-element.29), channel_id=1, source_target_pairs={{0,4},{4,0},{8,12},{12,8},{16,20},{20,16},{24,28},{28,24},{1,5},{5... | collective-permute-start | bytes 294920 | tf_op jit(solution)/shard_map/ppermute | solution.py:296
  17.3 14.2 %copy-start.1 = (f32[1,3,16,16,128]{4,3,2,1,0:T(8,128)S(1)}, f32[1,3,16,16,128]{4,3,2,1,0:T(8,128)}, u32[]{:S(2)}) copy-start(f32[1,3,16,16,128]{4,3,2,1,0:T(8,128)} %param.2) | copy-start | bytes 1179652
  17.3 6.5 %collective-permute-start.6 = (f32[4,3,2,8,128]{4,3,2,1,0:T(8,128)S(1)}, f32[4,3,2,8,128]{4,3,2,1,0:T(8,128)S(1)}, u32[]{:S(2)}, u32[]{:S(2)}) collective-permute-start(f32[4,3,2,8,128]{4,3,2,1,0:T(8,128)S(1)} %shard_map.32), channel_id=1, source_target_pairs={{0,24},{4,28},{8,16},{12,20},{16,8},{20,12},{24,0},{28,4},{1,25},{... | collective-permute-start | bytes 294920 | tf_op jit(solution)/shard_map/ppermute | solution.py:303
  24.0 5.9 %collective-permute-start.7 = (f32[4,3,2,8,128]{4,3,2,1,0:T(8,128)S(1)}, f32[4,3,2,8,128]{4,3,2,1,0:T(8,128)S(1)}, u32[]{:S(2)}, u32[]{:S(2)}) collective-permute-start(f32[4,3,2,8,128]{4,3,2,1,0:T(8,128)S(1)} %get-tuple-element.32), channel_id=1, source_target_pairs={{0,12},{4,8},{8,4},{12,0},{16,28},{20,24},{24,20},{28,16},{1,13},{... | collective-permute-start | bytes 294920 | tf_op jit(solution)/shard_map/ppermute | solution.py:296
  26.6 4.6 %collective-permute-start.8 = (f32[4,3,2,8,128]{4,3,2,1,0:T(8,128)S(1)}, f32[4,3,2,8,128]{4,3,2,1,0:T(8,128)S(1)}, u32[]{:S(2)}, u32[]{:S(2)}) collective-permute-start(f32[4,3,2,8,128]{4,3,2,1,0:T(8,128)S(1)} %get-tuple-element.33), channel_id=1, source_target_pairs={{0,8},{4,12},{8,0},{12,4},{16,24},{20,28},{24,16},{28,20},{1,9},{5... | collective-permute-start | bytes 294920 | tf_op jit(solution)/shard_map/ppermute | solution.py:296
  26.9 4.6 %collective-permute-start.9 = (f32[4,3,2,8,128]{4,3,2,1,0:T(8,128)S(1)}, f32[4,3,2,8,128]{4,3,2,1,0:T(8,128)S(1)}, u32[]{:S(2)}, u32[]{:S(2)}) collective-permute-start(f32[4,3,2,8,128]{4,3,2,1,0:T(8,128)S(1)} %get-tuple-element.34), channel_id=1, source_target_pairs={{0,4},{4,0},{8,12},{12,8},{16,20},{20,16},{24,28},{28,24},{1,5},{5... | collective-permute-start | bytes 294920 | tf_op jit(solution)/shard_map/ppermute | solution.py:296

commit v2 on v1

--- a/solution.py
+++ b/solution.py
@@ -36,8 +36,14 @@
     return jax.ShapeDtypeStruct(shape, jnp.float32)
 
 
+PARTNERS = ((1, 3, 2), (2, 3, 1))
+
+
 def partner(k):
-    return (GROUP - k) % GROUP
+    if k == 0:
+        return 0
+    odd = lax.rem(lax.axis_index("gz"), 2)
+    return jnp.where(odd == 1, PARTNERS[1][k - 1], PARTNERS[0][k - 1])
 
 
 def spot():
@@ -104,16 +110,12 @@
     return [[new[c][odd] + beta * base[c][odd] for odd in (0, 1)] for c in range(3)]
 
 
-def faces_kernel(own_ref, *refs):
-    *far_refs, near_ref = refs
-    layers, width, part = own_ref.shape[1], near_ref.shape[1], far_refs[0].shape[1]
+def faces_kernel(own_ref, far_ref, near_ref):
+    layers, width = own_ref.shape[1], near_ref.shape[1]
     near = near_side()
-    far = 1 - near
     top = layers - width
+    far_ref[...] = own_ref[:, pl.ds((1 - near) * top, width)]
     near_ref[...] = own_ref[:, pl.ds(near * top, width)]
-    for j, far_ref in enumerate(far_refs):
-        start = far * (top + j * part) + (1 - far) * (width - (j + 1) * part)
-        far_ref[...] = own_ref[:, pl.ds(start, part)]
 
 
 def inside_kernel(own_ref, rate_ref, edges, middle, faded, damp_ref, damps, *fields):
@@ -172,13 +174,12 @@
     damp_ref[...] = damps[side, pl.ds(lax.rem(chunk, 2) * share, share)]
 
 
-def border(side, faces, edges, middle, faded, jumps, strip):
+def border(side, face_ref, edges, middle, faded, jumps, strip):
     width = STAGES
     upward = 1.0 - 2.0 * side.astype(jnp.float32)
-    part = faces[0].shape[1]
     for slot in range(width):
-        layer = slot % part + side * (part - 1 - 2 * (slot % part))
-        store(strip, (0, slot), [split_rows(faces[slot // part], c, layer) for c in range(3)])
+        layer = slot + side * (width - 1 - 2 * slot)
+        store(strip, (0, slot), [split_rows(face_ref, c, layer) for c in range(3)])
 
     def at(stage, slot):
         if slot < width:
@@ -208,12 +209,12 @@
 
 
 def near_kernel(face_ref, edges, middle, faded, jumps, strip):
-    border(near_side(), [face_ref], edges, middle, faded, jumps, strip)
-
-
-def far_kernel(outer_ref, inner_ref, edges, middle, faded, near_jumps, *refs):
+    border(near_side(), face_ref, edges, middle, faded, jumps, strip)
+
+
+def far_kernel(face_ref, edges, middle, faded, near_jumps, *refs):
     outs, strip, jumps = refs[:GROUP], refs[GROUP], refs[GROUP + 1]
-    border(1 - near_side(), [outer_ref, inner_ref], edges, middle, faded, jumps.at[1], strip)
+    border(1 - near_side(), face_ref, edges, middle, faded, jumps.at[1], strip)
     jumps[0] = near_jumps[...]
     share = outs[0].shape[0]
     for k, out in enumerate(outs):
@@ -284,7 +285,7 @@
     layers, rows, width = own.shape[1:]
     half, share = layers // 2, layers // GROUP
     tile = (3, 2, rows // 2, width)
-    face, part = f32(3, STAGES, rows, width), f32(3, STAGES // 2, rows, width)
+    face = f32(3, STAGES, rows, width)
     piece = f32(share, *tile)
     team = lax.axis_index("tm") // GROUP
 
@@ -292,22 +293,24 @@
         return lax.ppermute(value, "gz", [(i, j % slabs) for i, j in pairs])
 
     def swap(parts):
-        return [parts[0]] + [
-            lax.ppermute(parts[k], "tm", [(i, i ^ partner(k)) for i in range(slices)])
-            for k in range(1, GROUP)
-        ]
+        moved = [parts[0]]
+        for k in range(1, GROUP):
+            pairs = [
+                (i * slabs + g, (i ^ PARTNERS[g % 2][k - 1]) * slabs + g)
+                for i in range(slices)
+                for g in range(slabs)
+            ]
+            moved.append(lax.ppermute(parts[k], ("tm", "gz"), pairs))
+        return moved
 
     def onward(value, distance):
         flip = 2 * (distance % 2)
         pairs = [(i, ((i ^ flip) + distance * GROUP) % slices) for i in range(slices)]
         return lax.ppermute(value, "tm", pairs)
 
-    *far_faces, near_face = call(faces_kernel, [part, part, face], own)
+    far_face, near_face = call(faces_kernel, [face, face], own)
     near_face = halo(near_face, [(i, i ^ 1) for i in range(slabs)])
-    far_faces = [
-        halo(face, [(i, i + 1 if i % 2 else i - 1 + slabs) for i in range(slabs)])
-        for face in far_faces
-    ]
+    far_face = halo(far_face, [(i, i + 1 if i % 2 else i - 1 + slabs) for i in range(slabs)])
     edges, middle, faded, damp = call(
         inside_kernel,
         [
@@ -326,7 +329,7 @@
         near_kernel, f32(half, *tile), near_face, edges, middle, faded, scratch=[strip], flops=1 << 24
     )
     jumps = call(
-        far_kernel, [piece] * GROUP, *far_faces, edges, middle, faded, near_jumps,
+        far_kernel, [piece] * GROUP, far_face, edges, middle, faded, near_jumps,
         scratch=[strip, pltpu.VMEM((2, half, *tile), jnp.float32)],
     )
     order = pltpu.VMEM((GROUP, *piece.shape), jnp.float32)

time: 32.4 us -> 32.9 us (1.015)
  waiting for transfers between devices: 14 us -> 15.6 us
  starting transfers between devices: 14 us -> 12.9 us
    ppermute x1, waiting for transfers between devices: 2.84 us -> 4.17 us  [onward(): return lax.ppermute(value, 'tm', pairs)]
    ppermute x1, starting transfers between devices: 3.7 us -> 2.61 us  [onward(): return lax.ppermute(value, 'tm', pairs)]
    ppermute x6, waiting for transfers between devices: 8.44 us -> 8.83 us  [swap(): moved.append(lax.ppermute(parts[k], ('tm', 'gz'), pairs))]
    ppermute x3 -> x2, waiting for transfers between devices: 2.74 us -> 2.56 us  [halo(): return lax.ppermute(value, 'gz', [(i, j % slabs) for i, j in pairs])]
    ppermute x3 -> x2, starting transfers between devices: 3.18 us -> 3.16 us  [halo(): return lax.ppermute(value, 'gz', [(i, j % slabs) for i, j in pairs])]
  transfers between devices with their start and end apart: 10 -> 9, of which waited for: 8 -> 6; matrix products, arithmetic and copies ran while one was open for 0% -> 0% of each run, Pallas kernels for 5% -> 5%
where the time goes in v2:
time: 32.9 us; the launch traced here: 32.7 us
  waiting for transfers between devices  15.6 us (47%)
  starting transfers between devices  12.9 us (39%)
  Pallas kernels  3.24 us (10%)
  local copies, waits for them, and re-layouts  1.01 us (3%)
    ppermute x6, waiting for transfers between devices, swap(): moved.append(lax.ppermute(parts[k], ('tm', 'gz'), pairs))  8.83 us
    ppermute x6, starting transfers between devices, swap(): moved.append(lax.ppermute(parts[k], ('tm', 'gz'), pairs))  7.11 us
    ppermute x1, waiting for transfers between devices, onward(): return lax.ppermute(value, 'tm', pairs)  4.17 us
    pallas_call x7, Pallas kernels, call(): pl.pallas_call(kernel, out_shape=out_shape, in_specs=[VMEM] * len(args),...  3.24 us
    ppermute x2, starting transfers between devices, halo(): return lax.ppermute(value, 'gz', [(i, j % slabs) for i, j in pairs])  3.16 us
    ppermute x1, starting transfers between devices, onward(): return lax.ppermute(value, 'tm', pairs)  2.61 us
    ppermute x2, waiting for transfers between devices, halo(): return lax.ppermute(value, 'gz', [(i, j % slabs) for i, j in pairs])  2.56 us
    unnamed x6, local copies, waits for them, and re-layouts  1.01 us
  transfers between devices with their start and end apart: 9, of which 6 were waited for; matrix products, arithmetic and copies ran while one was open for 0% of the time, Pallas kernels for 5%

profile of v2, /device:TPU:0, one launch (start us, length us, event | category | flops | bytes accessed | tf_op | source)
XLA Modules:
  0.0 32.7 jit_solution(298255518691184018)
XLA Ops:
  0.0 0.0 copy-start
  0.0 1.0 %copy-done = f32[1,3,16,16,128]{4,3,2,1,0:T(8,128)S(1)} copy-done((f32[1,3,16,16,128]{4,3,2,1,0:T(8,128)S(1)}, f32[1,3,16,16,128]{4,3,2,1,0:T(8,128)}, u32[]{:S(2)}) %copy-start) | copy-done | bytes 393240
  1.0 0.0 copy-start.2
  1.0 0.5 %collective-permute-start.1 = (f32[3,6,16,128]{3,2,1,0:T(8,128)S(1)}, f32[3,6,16,128]{3,2,1,0:T(8,128)S(1)}, u32[]{:S(2)}, u32[]{:S(2)}) collective-permute-start(f32[3,6,16,128]{3,2,1,0:T(8,128)S(1)} %get-tuple-element.23), channel_id=1, source_target_pairs={{0,1},{1,0},{2,3},{3,2},{4,5},{5,4},{6,7},{7,6},{8,9},{9,8},{10,11... | collective-permute-start | bytes 442376 | tf_op jit(solution)/shard_map/ppermute | solution.py:293
  1.5 2.6 %collective-permute-start = (f32[3,6,16,128]{3,2,1,0:T(8,128)S(1)}, f32[3,6,16,128]{3,2,1,0:T(8,128)S(1)}, u32[]{:S(2)}, u32[]{:S(2)}) collective-permute-start(f32[3,6,16,128]{3,2,1,0:T(8,128)S(1)} %get-tuple-element.19), channel_id=1, source_target_pairs={{0,3},{1,2},{2,1},{3,0},{4,7},{5,6},{6,5},{7,4},{8,11},{9,10},{10,... | collective-permute-start | bytes 442376 | tf_op jit(solution)/shard_map/ppermute | solution.py:293
  4.2 0.0 copy-done.2
  4.2 0.8 %shard_map.29 = (f32[6,2,3,3,2,8,128]{6,5,4,3,2,1,0:T(8,128)S(1)}, f32[2,2,3,2,8,128]{5,4,3,2,1,0:T(8,128)S(1)}, f32[2,6,3,2,8,128]{5,4,3,2,1,0:T(8,128)S(1)}, f32[4,2,8,128]{3,2,1,0:T(8,128)S(1)}) custom-call(f32[3,16,16,128]{3,2,1,0:T(8,128)S(1)} %bitcast.3, f32[16,16,128]{2,1,0:T(8,128)S(1)} %copy-done.2), custom_call_target="tpu_custom_call" | custom-call | flops 67108864 | bytes 1048576 | tf_op jit(solution)/shard_map/pallas_call | solution.py:24
  5.0 0.0 collective-permute-done.1.face_ref
  5.0 0.7 %shard_map.30.near_jumps = f32[8,3,2,8,128]{4,3,2,1,0:T(8,128)S(1)} custom-call(f32[3,6,16,128]{3,2,1,0:T(8,128)S(1)} %collective-permute-done.1.face_ref, f32[6,2,3,3,2,8,128]{6,5,4,3,2,1,0:T(8,128)S(1)} %get-tuple-element.20.edges, f32[2,2,3,2,8,128]{5,4,3,2,1,0:T(8,128)S(1)} %get-tuple-element.21.middle, f32[2,6,3,2,8,128]{5,4,3,2,1,0:T(8,128)S(1)} %get-tuple-element.22.faded), custom_call_target="tpu_custom_call" | custom-call | flops 16777216 | bytes 1048576 | tf_op jit(solution)/shard_map/pallas_call | solution.py:24
  5.8 2.6 %collective-permute-done.face_ref = f32[3,6,16,128]{3,2,1,0:T(8,128)S(1)} collective-permute-done((f32[3,6,16,128]{3,2,1,0:T(8,128)S(1)}, f32[3,6,16,128]{3,2,1,0:T(8,128)S(1)}, u32[]{:S(2)}, u32[]{:S(2)}) %collective-permute-start) | collective-permute-done | bytes 147488 | tf_op jit(solution)/shard_map/ppermute | solution.py:293
  8.3 0.7 %shard_map.31 = (f32[4,3,2,8,128]{4,3,2,1,0:T(8,128)S(1)}, f32[4,3,2,8,128]{4,3,2,1,0:T(8,128)S(1)}, f32[4,3,2,8,128]{4,3,2,1,0:T(8,128)S(1)}, f32[4,3,2,8,128]{4,3,2,1,0:T(8,128)S(1)}) custom-call(f32[3,6,16,128]{3,2,1,0:T(8,128)S(1)} %collective-permute-done.face_ref, f32[6,2,3,3,2,8,128]{6,5,4,3,2,1,0:T(8,128)S(1)} %get-tuple-element.20.edges, ...), custom_call_target="tpu_custom_call" | custom-call | tf_op jit(solution)/shard_map/pallas_call | solution.py:24
  9.0 1.4 %collective-permute-start.2 = (f32[4,3,2,8,128]{4,3,2,1,0:T(8,128)S(1)}, f32[4,3,2,8,128]{4,3,2,1,0:T(8,128)S(1)}, u32[]{:S(2)}, u32[]{:S(2)}) collective-permute-start(f32[4,3,2,8,128]{4,3,2,1,0:T(8,128)S(1)} %get-tuple-element.25), channel_id=1, source_target_pairs={{0,4},{1,9},{2,6},{3,11},{4,0},{5,13},{6,2},{7,15},{8,12},{9,1},{1... | collective-permute-start | bytes 294920 | tf_op jit(solution)/shard_map/ppermute | solution.py:303
  10.5 1.5 %collective-permute-start.3 = (f32[4,3,2,8,128]{4,3,2,1,0:T(8,128)S(1)}, f32[4,3,2,8,128]{4,3,2,1,0:T(8,128)S(1)}, u32[]{:S(2)}, u32[]{:S(2)}) collective-permute-start(f32[4,3,2,8,128]{4,3,2,1,0:T(8,128)S(1)} %get-tuple-element.26), channel_id=1, source_target_pairs={{0,12},{1,13},{2,14},{3,15},{4,8},{5,9},{6,10},{7,11},{8,4},{9,5},... | collective-permute-start | bytes 294920 | tf_op jit(solution)/shard_map/ppermute | solution.py:303
  12.0 0.6 %collective-permute-start.4 = (f32[4,3,2,8,128]{4,3,2,1,0:T(8,128)S(1)}, f32[4,3,2,8,128]{4,3,2,1,0:T(8,128)S(1)}, u32[]{:S(2)}, u32[]{:S(2)}) collective-permute-start(f32[4,3,2,8,128]{4,3,2,1,0:T(8,128)S(1)} %get-tuple-element.27), channel_id=1, source_target_pairs={{0,8},{1,5},{2,10},{3,7},{4,12},{5,1},{6,14},{7,3},{8,0},{9,13},{1... | collective-permute-start | bytes 294920 | tf_op jit(solution)/shard_map/ppermute | solution.py:303
  12.6 1.1 %collective-permute-done.2.refs_1_.refs_2_ = f32[4,3,2,8,128]{4,3,2,1,0:T(8,128)S(1)} collective-permute-done((f32[4,3,2,8,128]{4,3,2,1,0:T(8,128)S(1)}, f32[4,3,2,8,128]{4,3,2,1,0:T(8,128)S(1)}, u32[]{:S(2)}, u32[]{:S(2)}) %collective-permute-start.2) | collective-permute-done | bytes 98336 | tf_op jit(solution)/shard_map/ppermute | solution.py:303
  13.7 2.7 %collective-permute-done.3.refs_2_.refs_3_ = f32[4,3,2,8,128]{4,3,2,1,0:T(8,128)S(1)} collective-permute-done((f32[4,3,2,8,128]{4,3,2,1,0:T(8,128)S(1)}, f32[4,3,2,8,128]{4,3,2,1,0:T(8,128)S(1)}, u32[]{:S(2)}, u32[]{:S(2)}) %collective-permute-start.3) | collective-permute-done | bytes 98336 | tf_op jit(solution)/shard_map/ppermute | solution.py:303
  16.4 1.0 %collective-permute-done.4.refs_3_.refs_4_ = f32[4,3,2,8,128]{4,3,2,1,0:T(8,128)S(1)} collective-permute-done((f32[4,3,2,8,128]{4,3,2,1,0:T(8,128)S(1)}, f32[4,3,2,8,128]{4,3,2,1,0:T(8,128)S(1)}, u32[]{:S(2)}, u32[]{:S(2)}) %collective-permute-start.4) | collective-permute-done | bytes 98336 | tf_op jit(solution)/shard_map/ppermute | solution.py:303
  17.3 0.1 shard_map.32
  17.4 0.0 copy-start.1
  17.4 2.6 %collective-permute-start.5 = (f32[4,3,2,8,128]{4,3,2,1,0:T(8,128)S(1)}, f32[4,3,2,8,128]{4,3,2,1,0:T(8,128)S(1)}, u32[]{:S(2)}, u32[]{:S(2)}) collective-permute-start(f32[4,3,2,8,128]{4,3,2,1,0:T(8,128)S(1)} %shard_map.32), channel_id=1, source_target_pairs={{0,24},{4,28},{8,16},{12,20},{16,8},{20,12},{24,0},{28,4},{1,25},{... | collective-permute-start | bytes 294920 | tf_op jit(solution)/shard_map/ppermute | solution.py:309
  20.0 4.2 %collective-permute-done.5.refs_0_ = f32[4,3,2,8,128]{4,3,2,1,0:T(8,128)S(1)} collective-permute-done((f32[4,3,2,8,128]{4,3,2,1,0:T(8,128)S(1)}, f32[4,3,2,8,128]{4,3,2,1,0:T(8,128)S(1)}, u32[]{:S(2)}, u32[]{:S(2)}) %collective-permute-start.5) | collective-permute-done | bytes 98336 | tf_op jit(solution)/shard_map/ppermute | solution.py:309
  24.2 0.1 shard_map.33
  24.3 0.9 %collective-permute-start.6 = (f32[4,3,2,8,128]{4,3,2,1,0:T(8,128)S(1)}, f32[4,3,2,8,128]{4,3,2,1,0:T(8,128)S(1)}, u32[]{:S(2)}, u32[]{:S(2)}) collective-permute-start(f32[4,3,2,8,128]{4,3,2,1,0:T(8,128)S(1)} %get-tuple-element.30), channel_id=1, source_target_pairs={{0,4},{1,9},{2,6},{3,11},{4,0},{5,13},{6,2},{7,15},{8,12},{9,1},{1... | collective-permute-start | bytes 294920 | tf_op jit(solution)/shard_map/ppermute | solution.py:303
  25.2 2.2 %collective-permute-start.7 = (f32[4,3,2,8,128]{4,3,2,1,0:T(8,128)S(1)}, f32[4,3,2,8,128]{4,3,2,1,0:T(8,128)S(1)}, u32[]{:S(2)}, u32[]{:S(2)}) collective-permute-start(f32[4,3,2,8,128]{4,3,2,1,0:T(8,128)S(1)} %get-tuple-element.31), channel_id=1, source_target_pairs={{0,12},{1,13},{2,14},{3,15},{4,8},{5,9},{6,10},{7,11},{8,4},{9,5},... | collective-permute-start | bytes 294920 | tf_op jit(solution)/shard_map/ppermute | solution.py:303
  27.3 0.5 %collective-permute-start.8 = (f32[4,3,2,8,128]{4,3,2,1,0:T(8,128)S(1)}, f32[4,3,2,8,128]{4,3,2,1,0:T(8,128)S(1)}, u32[]{:S(2)}, u32[]{:S(2)}) collective-permute-start(f32[4,3,2,8,128]{4,3,2,1,0:T(8,128)S(1)} %get-tuple-element.32), channel_id=1, source_target_pairs={{0,8},{1,5},{2,10},{3,7},{4,12},{5,1},{6,14},{7,3},{8,0},{9,13},{1... | collective-permute-start | bytes 294920 | tf_op jit(solution)/shard_map/ppermute | solution.py:303
  27.9 4.0 %collective-permute-done.6.refs_1_ = f32[4,3,2,8,128]{4,3,2,1,0:T(8,128)S(1)} collective-permute-done((f32[4,3,2,8,128]{4,3,2,1,0:T(8,128)S(1)}, f32[4,3,2,8,128]{4,3,2,1,0:T(8,128)S(1)}, u32[]{:S(2)}, u32[]{:S(2)}) %collective-permute-start.6) | collective-permute-done | bytes 98336 | tf_op jit(solution)/shard_map/ppermute | solution.py:303
  31.9 0.0 collective-permute-done.7.refs_2_
  31.9 0.0 collective-permute-done.8.refs_3_
  32.0 0.0 copy-done.1
  32.0 0.8 %shard_map.34 = f32[3,16,16,128]{3,2,1,0:T(8,128)} custom-call(f32[3,16,16,128]{3,2,1,0:T(8,128)S(1)} %bitcast.4, f32[4,3,2,8,128]{4,3,2,1,0:T(8,128)S(1)} %get-tuple-element.29.refs_0_, f32[4,3,2,8,128]{4,3,2,1,0:T(8,128)S(1)} %collective-permute-done.6.refs_1_, f32[4,3,2,8,128]{4,3,2,1,0:T(8,128)S(1)} %collective-permute-done.7.refs_2_, ...), custom_call_target="tpu_custom_call" | custom-call | tf_op jit(solution)/shard_map/pallas_call | solution.py:24
  (1 shorter events, 0.0 us)
Async XLA Ops:
  0.0 1.0 %copy-start = (f32[1,3,16,16,128]{4,3,2,1,0:T(8,128)S(1)}, f32[1,3,16,16,128]{4,3,2,1,0:T(8,128)}, u32[]{:S(2)}) copy-start(f32[1,3,16,16,128]{4,3,2,1,0:T(8,128)} %param.2) | copy-start | bytes 1179652
  1.0 3.2 %copy-start.2 = (f32[16,16,128]{2,1,0:T(8,128)S(1)}, f32[16,16,128]{2,1,0:T(8,128)}, u32[]{:S(2)}) copy-start(f32[16,16,128]{2,1,0:T(8,128)} %rate_ref.1) | copy-start | bytes 393220
  1.0 4.0 %collective-permute-start.1 = (f32[3,6,16,128]{3,2,1,0:T(8,128)S(1)}, f32[3,6,16,128]{3,2,1,0:T(8,128)S(1)}, u32[]{:S(2)}, u32[]{:S(2)}) collective-permute-start(f32[3,6,16,128]{3,2,1,0:T(8,128)S(1)} %get-tuple-element.23), channel_id=1, source_target_pairs={{0,1},{1,0},{2,3},{3,2},{4,5},{5,4},{6,7},{7,6},{8,9},{9,8},{10,11... | collective-permute-start | bytes 442376 | tf_op jit(solution)/shard_map/ppermute | solution.py:293
  1.5 6.8 %collective-permute-start = (f32[3,6,16,128]{3,2,1,0:T(8,128)S(1)}, f32[3,6,16,128]{3,2,1,0:T(8,128)S(1)}, u32[]{:S(2)}, u32[]{:S(2)}) collective-permute-start(f32[3,6,16,128]{3,2,1,0:T(8,128)S(1)} %get-tuple-element.19), channel_id=1, source_target_pairs={{0,3},{1,2},{2,1},{3,0},{4,7},{5,6},{6,5},{7,4},{8,11},{9,10},{10,... | collective-permute-start | bytes 442376 | tf_op jit(solution)/shard_map/ppermute | solution.py:293
  9.0 4.7 %collective-permute-start.2 = (f32[4,3,2,8,128]{4,3,2,1,0:T(8,128)S(1)}, f32[4,3,2,8,128]{4,3,2,1,0:T(8,128)S(1)}, u32[]{:S(2)}, u32[]{:S(2)}) collective-permute-start(f32[4,3,2,8,128]{4,3,2,1,0:T(8,128)S(1)} %get-tuple-element.25), channel_id=1, source_target_pairs={{0,4},{1,9},{2,6},{3,11},{4,0},{5,13},{6,2},{7,15},{8,12},{9,1},{1... | collective-permute-start | bytes 294920 | tf_op jit(solution)/shard_map/ppermute | solution.py:303
  10.5 5.9 %collective-permute-start.3 = (f32[4,3,2,8,128]{4,3,2,1,0:T(8,128)S(1)}, f32[4,3,2,8,128]{4,3,2,1,0:T(8,128)S(1)}, u32[]{:S(2)}, u32[]{:S(2)}) collective-permute-start(f32[4,3,2,8,128]{4,3,2,1,0:T(8,128)S(1)} %get-tuple-element.26), channel_id=1, source_target_pairs={{0,12},{1,13},{2,14},{3,15},{4,8},{5,9},{6,10},{7,11},{8,4},{9,5},... | collective-permute-start | bytes 294920 | tf_op jit(solution)/shard_map/ppermute | solution.py:303
  12.0 5.3 %collective-permute-start.4 = (f32[4,3,2,8,128]{4,3,2,1,0:T(8,128)S(1)}, f32[4,3,2,8,128]{4,3,2,1,0:T(8,128)S(1)}, u32[]{:S(2)}, u32[]{:S(2)}) collective-permute-start(f32[4,3,2,8,128]{4,3,2,1,0:T(8,128)S(1)} %get-tuple-element.27), channel_id=1, source_target_pairs={{0,8},{1,5},{2,10},{3,7},{4,12},{5,1},{6,14},{7,3},{8,0},{9,13},{1... | collective-permute-start | bytes 294920 | tf_op jit(solution)/shard_map/ppermute | solution.py:303
  17.4 14.5 %copy-start.1 = (f32[1,3,16,16,128]{4,3,2,1,0:T(8,128)S(1)}, f32[1,3,16,16,128]{4,3,2,1,0:T(8,128)}, u32[]{:S(2)}) copy-start(f32[1,3,16,16,128]{4,3,2,1,0:T(8,128)} %param.2) | copy-start | bytes 1179652
  17.4 6.8 %collective-permute-start.5 = (f32[4,3,2,8,128]{4,3,2,1,0:T(8,128)S(1)}, f32[4,3,2,8,128]{4,3,2,1,0:T(8,128)S(1)}, u32[]{:S(2)}, u32[]{:S(2)}) collective-permute-start(f32[4,3,2,8,128]{4,3,2,1,0:T(8,128)S(1)} %shard_map.32), channel_id=1, source_target_pairs={{0,24},{4,28},{8,16},{12,20},{16,8},{20,12},{24,0},{28,4},{1,25},{... | collective-permute-start | bytes 294920 | tf_op jit(solution)/shard_map/ppermute | solution.py:309
  24.3 7.6 %collective-permute-start.6 = (f32[4,3,2,8,128]{4,3,2,1,0:T(8,128)S(1)}, f32[4,3,2,8,128]{4,3,2,1,0:T(8,128)S(1)}, u32[]{:S(2)}, u32[]{:S(2)}) collective-permute-start(f32[4,3,2,8,128]{4,3,2,1,0:T(8,128)S(1)} %get-tuple-element.30), channel_id=1, source_target_pairs={{0,4},{1,9},{2,6},{3,11},{4,0},{5,13},{6,2},{7,15},{8,12},{9,1},{1... | collective-permute-start | bytes 294920 | tf_op jit(solution)/shard_map/ppermute | solution.py:303
  25.2 6.7 %collective-permute-start.7 = (f32[4,3,2,8,128]{4,3,2,1,0:T(8,128)S(1)}, f32[4,3,2,8,128]{4,3,2,1,0:T(8,128)S(1)}, u32[]{:S(2)}, u32[]{:S(2)}) collective-permute-start(f32[4,3,2,8,128]{4,3,2,1,0:T(8,128)S(1)} %get-tuple-element.31), channel_id=1, source_target_pairs={{0,12},{1,13},{2,14},{3,15},{4,8},{5,9},{6,10},{7,11},{8,4},{9,5},... | collective-permute-start | bytes 294920 | tf_op jit(solution)/shard_map/ppermute | solution.py:303
  27.3 4.6 %collective-permute-start.8 = (f32[4,3,2,8,128]{4,3,2,1,0:T(8,128)S(1)}, f32[4,3,2,8,128]{4,3,2,1,0:T(8,128)S(1)}, u32[]{:S(2)}, u32[]{:S(2)}) collective-permute-start(f32[4,3,2,8,128]{4,3,2,1,0:T(8,128)S(1)} %get-tuple-element.32), channel_id=1, source_target_pairs={{0,8},{1,5},{2,10},{3,7},{4,12},{5,1},{6,14},{7,3},{8,0},{9,13},{1... | collective-permute-start | bytes 294920 | tf_op jit(solution)/shard_map/ppermute | solution.py:303
